TPU v7x, 32 devices: a whole 2x2x4 slice. The times are simulated.
32 devices in a mesh: lon: 8 (over y, x, core), lat: 4 (over z).
Axes of the slice: x: 2, y: 2, z: 4, core: 2. Of those that a mesh axis runs over, the one named last changes fastest.
Arguments:
- eta_init: float32 [2, 512, 8192], P(None, 'lat', 'lon'), may hold values from -6 to 6
- depth: float32 [512, 8192], P('lat', 'lon'), may hold values from 0.1 to 1
- sea_mask: int32 [512, 8192], P('lat', 'lon'), may hold values 0 or 1
- probe_cells: int32 [32, 2, 192], P(('lon', 'lat')), may hold values from 0 to 8191, as said below
- elapsed_record: bfloat16 [32, 2, 192, 1024], P(('lon', 'lat')), may hold values from -6 to 6
- gauge_kernels: bfloat16 [32, 32, 192, 1024], P(('lon', 'lat')), may hold values from -0.013671875 to 0.013671875
Outputs:
- eta_final: float32 [2, 512, 8192], P(None, 'lat', 'lon')
- shore_outlook: float32 [32, 2, 8, 32], P(('lon', 'lat'))
Inputs may be any that keep to these rules, and one draw needn't show every extreme that they name: probe_cells[g, 0, k] is a row below 512 and probe_cells[g, 1, k] a column below 8192. All probes of segment g lie in latitude band b = g % 4, rows 128 * b to 128 * b + 127. Of one segment's 192 probes at most 32 lie in one longitude sector of 1024 columns, and every segment has exactly 32 in some sector.
All inputs are finite; a program needn't handle non-finite values. No bound on the sum of `sea_mask` on one device may be relied on, other than what follows from the above.
Results may differ from a plain program's by a relative error of at most 0.0003.
Values sent between devices are 32-bit elements; how exact they have to be, the bound alone decides.
No kernel may reach another device: no remote copies, remote signals or barrier semaphores. Data moves between devices by JAX's collectives and lax.ppermute only.
A program may use at most 192 MiB of HBM per device.

v0:
```python
import functools
import math

import jax
import jax.numpy as jnp
from jax import lax
from jax.experimental import pallas as pl
from jax.experimental.pallas import tpu as pltpu
from jax.sharding import PartitionSpec as P

STEPS = 8
CAP = 32
LANES = 128
SUB = 8
HALO = 8
KTILE = 16
GROUP = 32
DEEP = 5
PITCH = 136
MIB = 1024 * 1024


def courant_for(total_lat, spacing):
    coldest = math.cos(0.5 * total_lat * spacing)
    return 0.95 * coldest / math.sqrt(1.0 + coldest * coldest)


def nt(a, b, precision=None):
    return lax.dot_general(
        a, b, (((1,), (1,)), ((), ())), preferred_element_type=jnp.float32, precision=precision
    )


def iota(shape, axis):
    return lax.broadcasted_iota(jnp.int32, shape, axis)


def lanes_between(lane, low, width):
    return (lane >= low) & (lane < low + width)


def rows_kernel(members, eta_ref, dep_ref, sea_ref, first_ref, last_ref, eta, dep, sea, sems):
    rows = eta_ref.shape[1]
    tiles = eta_ref.shape[2] // LANES
    copies = []
    for side, row in ((0, 0), (1, rows - HALO)):
        for k, (src, dst) in enumerate(
            (
                (eta_ref.at[:, pl.ds(row, HALO), :], eta.at[side]),
                (dep_ref.at[pl.ds(row, HALO), :], dep.at[side]),
                (sea_ref.at[pl.ds(row, HALO), :], sea.at[side]),
            )
        ):
            copy = pltpu.make_async_copy(src, dst, sems.at[side, k])
            copy.start()
            copies.append(copy)
    for copy in copies:
        copy.wait()
    for side, out in ((0, first_ref), (1, last_ref)):
        for t in range(tiles):
            at = slice(t * LANES, (t + 1) * LANES)
            wet = sea[side, :, at].astype(jnp.float32)
            for m in range(members):
                out[pl.ds(m * HALO * tiles + t, HALO, stride=tiles), :] = eta[side, m, :, at] * wet
            out[pl.ds(members * HALO * tiles + t, HALO, stride=tiles), :] = dep[side, :, at] * wet


def place_strip(lane, block, west, east):
    base = (block // DEEP) * GROUP
    one = jnp.zeros(lane.shape, jnp.float32)
    two = jnp.zeros(lane.shape, jnp.float32)
    for i in range(len(west)):
        low = base + i * HALO
        here = lanes_between(lane, low, HALO)
        one = jnp.where(here, pltpu.roll(west[i], low, axis=1) if low else west[i], one)
        two = jnp.where(here, pltpu.roll(east[i], (low + HALO) % LANES, axis=1), two)
    return one, two


def table_kernel(
    lat_cells, lon_cells, lat_count, lon_count, members,
    cells_ref, eta_ref, dep_ref, sea_ref, msg_ref, one_ref, two_ref, own_ref, pick_ref, eta, dep, sea, sems,
):
    tiles = lon_cells // LANES
    copies = []
    for side, col in ((0, 0), (1, lon_cells - LANES)):
        for k, (src, dst) in enumerate(
            (
                (eta_ref.at[:, :, pl.ds(col, LANES)], eta.at[side]),
                (dep_ref.at[:, pl.ds(col, LANES)], dep.at[side]),
                (sea_ref.at[:, pl.ds(col, LANES)], sea.at[side]),
            )
        ):
            copy = pltpu.make_async_copy(src, dst, sems.at[side, k])
            copy.start()
            copies.append(copy)

    probes = cells_ref.shape[1]
    rows = cells_ref[0:1, :]
    cols = cells_ref[1:2, :]
    for band in range(lat_count - 1, 0, -1):
        rows = rows - jnp.where(rows >= band * lat_cells, lat_cells, 0)
    sector = jnp.zeros_like(cols)
    for s in range(1, lon_count):
        sector = sector + jnp.where(cols >= s * lon_cells, 1, 0)
    cols = cols - sector * lon_cells
    tile = jnp.zeros_like(cols)
    for t in range(1, tiles):
        tile = tile + jnp.where(cols >= t * LANES, 1, 0)
    lane = cols - tile * LANES
    low = cols < HALO
    high = cols >= lon_cells - HALO
    lane = jnp.where(low, LANES - 2 * HALO + cols, lane)
    lane = jnp.where(high, cols - (lon_cells - 2 * HALO), lane)
    main = (HALO + rows) * tiles + tile
    rim = (lat_cells + 2 * HALO) * tiles + HALO + rows
    place = jnp.where(low | high, rim, main)
    code = (place - HALO * tiles) * LANES + lane
    hits = (iota((lon_count, probes), 0) == sector).astype(jnp.float32)
    before = (iota((probes, probes), 0) < iota((probes, probes), 1)).astype(jnp.float32)
    counts = lax.dot_general(
        hits.astype(jnp.bfloat16),
        before.astype(jnp.bfloat16),
        (((1,), (0,)), ((), ())),
        preferred_element_type=jnp.float32,
    )
    rank = jnp.sum(hits * counts, axis=0, keepdims=True)
    slots = lon_count * CAP
    key = sector * CAP + rank.astype(jnp.int32)
    pick = (iota((slots, probes), 0) == key).astype(jnp.float32).astype(jnp.bfloat16)
    pick_ref[...] = pick
    digit_row = iota((SUB, probes), 0)
    digits = jnp.where(digit_row == 0, code & 255, 0)
    digits = jnp.where(digit_row == 1, (code >> 8) & 255, digits)
    digits = jnp.where(digit_row == 2, code >> 16, digits)
    sent = nt(digits.astype(jnp.float32).astype(jnp.bfloat16), pick)
    sent = (sent[0:1] + 256.0 * sent[1:2] + 65536.0 * sent[2:3]).astype(jnp.int32)
    msg_ref[...] = jnp.zeros_like(msg_ref)
    for s in range(lon_count):
        msg_ref[s, :, 0:CAP] = sent[:, s * CAP : (s + 1) * CAP]

    for copy in copies:
        copy.wait()
    lane = iota((SUB, LANES), 1)
    zero = jnp.zeros((SUB, LANES), jnp.float32)
    total = lat_cells + 2 * HALO
    one = [zero] * DEEP
    two = [zero] * DEEP
    for blk in range(lat_cells // SUB):
        at = slice(blk * SUB, (blk + 1) * SUB)
        wet = [sea[side, at, :].astype(jnp.float32) for side in range(2)]
        west, east = (
            [eta[side, m, at, :] * wet[side] for m in range(members)] + [dep[side, at, :] * wet[side]]
            for side in range(2)
        )
        block = blk + HALO // SUB
        a, b = place_strip(lane, block, west, east)
        here = lanes_between(lane, (block // DEEP) * GROUP, GROUP)
        one[block % DEEP] = jnp.where(here, a, one[block % DEEP])
        two[block % DEEP] = jnp.where(here, b, two[block % DEEP])
        for i in range(members + 1):
            v = jnp.where(lane < 2 * HALO, pltpu.roll(east[i], 2 * HALO, axis=1), 0.0)
            v = jnp.where(lane >= LANES - 2 * HALO, pltpu.roll(west[i], LANES - 2 * HALO, axis=1), v)
            own_ref[i * total + HALO + blk * SUB : i * total + HALO + (blk + 1) * SUB, :] = v
    for d in range(DEEP):
        one_ref[d * SUB : (d + 1) * SUB, :] = one[d]
        two_ref[d * SUB : (d + 1) * SUB, :] = two[d]


def rim_kernel(members, odd_ref, one_ref, two_ref, top_ref, bot_ref, a_ref, b_ref):
    tiles = top_ref.shape[0] // ((members + 1) * HALO)
    lane = iota((SUB, LANES), 1)
    odd = odd_ref[0] == 1
    one = [one_ref[d * SUB : (d + 1) * SUB, :] for d in range(DEEP)]
    two = [two_ref[d * SUB : (d + 1) * SUB, :] for d in range(DEEP)]
    for ref, block in ((top_ref, 0), (bot_ref, DEEP * (LANES // GROUP) - 3)):
        west, east = (
            [ref[pl.ds(i * HALO * tiles + t, HALO, stride=tiles), :] for i in range(members + 1)]
            for t in (0, tiles - 1)
        )
        v, w = place_strip(lane, block, west, east)
        here = lanes_between(lane, (block // DEEP) * GROUP, (members + 1) * HALO)
        d = block % DEEP
        one[d] = jnp.where(here, v, one[d])
        two[d] = jnp.where(here, w, two[d])
    for d in range(DEEP):
        a_ref[d * SUB : (d + 1) * SUB, :] = jnp.where(odd, one[d], two[d])
        b_ref[d * SUB : (d + 1) * SUB, :] = jnp.where(odd, two[d], one[d])


def wave_kernel(
    members, stride, odd_ref, idx_ref, eta_ref, dep_ref, sea_ref, top_ref, bot_ref, a_ref, b_ref, own_ref, fac_ref,
    out_ref, smp_ref, eta, dep, sea, wet, ce, cn, rim_wet, rim_ce, rim_cn, out, sems, out_sems, *rest,
):
    hist = rest[:members]
    east = rest[members : 2 * members]
    north = rest[2 * members : 3 * members]
    rim_east = rest[3 * members : 4 * members]
    rim_north = rest[4 * members : 5 * members]
    rows = eta_ref.shape[1]
    tiles = eta_ref.shape[2] // LANES
    total = rows + 2 * HALO
    blocks = total // SUB
    rim = total * tiles
    lane = iota((SUB, LANES), 1)
    row8 = iota((SUB, LANES), 0)
    last = lane == LANES - 1
    first = lane == 0
    odd = odd_ref[0] == 1
    zero = jnp.zeros((SUB, LANES), jnp.float32)

    copies = []
    for t in range(tiles):
        cols = pl.ds(t * LANES, LANES)
        for m in range(members):
            copies.append((eta_ref.at[m, :, cols], eta.at[pl.ds((m * tiles + t) * PITCH, rows), :]))
        copies.append((dep_ref.at[:, cols], dep.at[pl.ds(t * PITCH, rows), :]))
        copies.append((sea_ref.at[:, cols], sea.at[pl.ds(t * PITCH, rows), :]))
    copies = [pltpu.make_async_copy(a, b, sems.at[k]) for k, (a, b) in enumerate(copies)]
    for copy in copies:
        copy.start()

    def shl(v):
        v = pltpu.roll(v, LANES - 1, axis=1)
        return jnp.where(last, pltpu.roll(v, SUB - 1, axis=0), v)

    def shr(v):
        v = pltpu.roll(v, 1, axis=1)
        return jnp.where(first, pltpu.roll(v, 1, axis=0), v)

    def vec(r):
        return slice(r * tiles, (r + 1) * tiles)

    def blk(b):
        return slice(b * SUB, (b + 1) * SUB)

    def fac(k, r):
        return fac_ref[k * total + r : k * total + r + 1, :]

    for b in range(blocks):
        d = b % DEEP
        base = (b // DEEP) * GROUP
        one = a_ref[blk(d), :]
        two = b_ref[blk(d), :]
        from_left = jnp.where(odd, one, two)
        from_right = jnp.where(odd, two, one)
        for i in range(members + 1):
            if b == 0 or b == blocks - 1:
                ref = top_ref if b == 0 else bot_ref
                w = ref[pl.ds(i * HALO * tiles, HALO, stride=tiles), :]
                e = ref[pl.ds(i * HALO * tiles + tiles - 1, HALO, stride=tiles), :]
                v = jnp.where(lane < 2 * HALO, pltpu.roll(e, 2 * HALO, axis=1), 0.0)
                v = jnp.where(lane >= LANES - 2 * HALO, pltpu.roll(w, LANES - 2 * HALO, axis=1), v)
            else:
                v = own_ref[i * total + b * SUB : i * total + (b + 1) * SUB, :]
            low = base + i * HALO
            far = pltpu.roll(from_right, (2 * HALO - low) % LANES, axis=1)
            v = jnp.where(lanes_between(lane, 2 * HALO, HALO), far, v)
            far = pltpu.roll(from_left, (LANES - 3 * HALO - low) % LANES, axis=1)
            v = jnp.where(lanes_between(lane, LANES - 3 * HALO, HALO), far, v)
            if i < members:
                hist[i][rim + b * SUB : rim + (b + 1) * SUB, :] = v
            else:
                rim_wet[blk(b), :] = v
    rim_wet[blk(blocks), :] = zero
    for q in range(STEPS):
        for m in range(members):
            at = q * stride + rim + total
            hist[m][at : at + SUB, :] = zero
    for b in range(blocks):
        w = rim_wet[blk(b), :]
        below = rim_wet[b * SUB + 1 : (b + 1) * SUB + 1, :]
        rim_ce[blk(b), :] = fac_ref[blk(b), :] * jnp.sqrt(w * pltpu.roll(w, LANES - 1, axis=1))
        rim_cn[blk(b), :] = fac_ref[total + b * SUB : total + (b + 1) * SUB, :] * jnp.sqrt(w * below)

    for ref, row in ((top_ref, 0), (bot_ref, rows + HALO)):
        size = HALO * tiles
        for m in range(members):
            hist[m][row * tiles : row * tiles + size, :] = ref[m * size : (m + 1) * size, :]
        wet[row * tiles : row * tiles + size, :] = ref[members * size : (members + 1) * size, :]
    for copy in copies:
        copy.wait()
    for r in range(rows):
        here = sea[pl.ds(r, tiles, stride=PITCH), :].astype(jnp.float32)
        for m in range(members):
            hist[m][vec(r + HALO), :] = eta[pl.ds(m * tiles * PITCH + r, tiles, stride=PITCH), :] * here
        wet[vec(r + HALO), :] = dep[pl.ds(r, tiles, stride=PITCH), :] * here
    w = wet[vec(0), :]
    for r in range(total - 1):
        below = wet[vec(r + 1), :]
        ce[vec(r), :] = fac(0, r) * jnp.sqrt(w * shl(w))
        cn[vec(r), :] = fac(1, r) * jnp.sqrt(w * below)
        w = below

    for q in range(STEPS):
        low, high = q + 1, total - 1 - q
        base = q * stride
        after = base + stride
        s, above = [], []
        for m in range(members):
            before = hist[m][base + (low - 1) * tiles : base + low * tiles, :]
            s.append(hist[m][base + low * tiles : base + (low + 1) * tiles, :])
            n = s[m] - before
            if q:
                n = north[m][vec(low - 1), :] + n
            above.append(cn[vec(low - 1), :] * n)
        rim_above = [zero] * members

        def rim_block(b):
            scale = fac_ref[2 * total + b * SUB : 2 * total + (b + 1) * SUB, :]
            for m in range(members):
                at = base + rim + b * SUB
                v = hist[m][at : at + SUB, :]
                below = hist[m][at + 1 : at + SUB + 1, :]
                e = pltpu.roll(v, LANES - 1, axis=1) - v
                n = below - v
                if q:
                    e = rim_east[m][blk(b), :] + e
                    n = rim_north[m][blk(b), :] + n
                fe = rim_ce[blk(b), :] * e
                fn = rim_cn[blk(b), :] * n
                if q < STEPS - 1:
                    rim_east[m][blk(b), :] = e
                    rim_north[m][blk(b), :] = n
                moved = pltpu.roll(fn, 1, axis=0)
                upper = jnp.where(row8 == 0, rim_above[m], moved)
                rim_above[m] = moved
                at = at + stride
                hist[m][at : at + SUB, :] = v + ((fe - pltpu.roll(fe, 1, axis=1)) + scale * (fn - upper))

        for r in range(low, high):
            if r % SUB == 0:
                rim_block(r // SUB - 1)
            scale = fac(2, r)
            to_east = ce[vec(r), :]
            to_north = cn[vec(r), :]
            for m in range(members):
                below = hist[m][base + (r + 1) * tiles : base + (r + 2) * tiles, :]
                e = shl(s[m]) - s[m]
                n = below - s[m]
                if q:
                    e = east[m][vec(r), :] + e
                    n = north[m][vec(r), :] + n
                fe = to_east * e
                fn = to_north * n
                if q < STEPS - 1:
                    east[m][vec(r), :] = e
                    north[m][vec(r), :] = n
                hist[m][after + r * tiles : after + (r + 1) * tiles, :] = s[m] + (
                    (fe - shr(fe)) + scale * (fn - above[m])
                )
                s[m] = below
                above[m] = fn
        for b in range((high - 1) // SUB, blocks):
            rim_block(b)

    copies = []
    end = STEPS * stride
    for m in range(members):
        for b in range(rows // SUB):
            at = end + rim + HALO + b * SUB
            edge = hist[m][at : at + SUB, :]
            for t in range(tiles):
                v = hist[m][pl.ds(end + (HALO + b * SUB) * tiles + t, SUB, stride=tiles), :]
                if t == 0:
                    v = jnp.where(lane < HALO, pltpu.roll(edge, 2 * HALO, axis=1), v)
                if t == tiles - 1:
                    v = jnp.where(lane >= LANES - HALO, pltpu.roll(edge, LANES - 2 * HALO, axis=1), v)
                out[m, blk(b), t * LANES : (t + 1) * LANES] = v
        copy = pltpu.make_async_copy(out.at[m], out_ref.at[m], out_sems.at[m])
        copy.start()
        copies.append(copy)

    def sample(s, carry):
        acc = zero
        for j in range(CAP):
            code = idx_ref[s, 0, j]
            spot = lax.bitwise_and(code, LANES - 1)
            place = lax.shift_right_logical(code, 7) + (stride + HALO * tiles)
            for m in range(members):
                v = hist[m][pl.ds(place, STEPS, stride=stride), :]
                target = m * CAP + j
                v = pltpu.roll(v, lax.bitwise_and(target - spot, LANES - 1), axis=1)
                acc = jnp.where(lane == target, v, acc)
        smp_ref[s] = acc
        return carry

    lax.fori_loop(0, smp_ref.shape[0], sample, 0)
    for copy in copies:
        copy.wait()


def past_kernel(members, g_ref, e_ref, out_ref, g, e, sems):
    coast, probes, lag_count = g_ref.shape[1:]
    parts = probes // KTILE
    copies = [pltpu.make_async_copy(e_ref.at[0], e, sems.at[parts])]
    for k in range(parts):
        at = pl.ds(k * KTILE, KTILE)
        copies.append(pltpu.make_async_copy(g_ref.at[0, :, at, :], g.at[k], sems.at[k]))
    for copy in copies:
        copy.start()
    copies[0].wait()
    lane = iota((members * KTILE, LANES), 1)

    def windows(k):
        past = e[:, k * KTILE : (k + 1) * KTILE, :].reshape(members * KTILE, lag_count).astype(jnp.float32)
        shifted = []
        for t in range(1, STEPS + 1):
            moved = pltpu.roll(past, t, axis=1)
            start = jnp.where(lane >= t, moved[:, :LANES], 0.0)
            shifted.append(jnp.concatenate([start, moved[:, LANES:]], axis=1).astype(jnp.bfloat16))
        return jnp.concatenate(shifted, axis=0)

    acc = None
    for k in range(0, parts, 2):
        w = jnp.concatenate([windows(k), windows(k + 1)], axis=1)
        copies[1 + k].wait()
        copies[2 + k].wait()
        x = jnp.concatenate([g[k + i].reshape(coast * KTILE, lag_count) for i in range(2)], axis=1)
        part = nt(x, w)
        acc = part if acc is None else acc + part
    same = (iota(acc.shape, 0) & (KTILE - 1)) == (iota(acc.shape, 1) & (KTILE - 1))
    kept = jnp.sum(jnp.where(same, acc, 0.0).reshape(coast, KTILE, acc.shape[1]), axis=1)
    wins = members * STEPS
    row = iota((wins, acc.shape[1]), 0)
    col = iota((wins, acc.shape[1]), 1)
    fold = ((col // KTILE) == (row & (STEPS - 1)) * members + row // STEPS).astype(jnp.float32)
    out_ref[...] = nt(fold, kept, precision=lax.Precision.HIGHEST)


def recent_kernel(g_ref, pick_ref, out_ref, lags_ref):
    coast = g_ref.shape[0]
    probes = g_ref.shape[1]
    first = (iota((SUB, LANES), 0) == iota((SUB, LANES), 1)).astype(jnp.float32).astype(jnp.bfloat16)
    for c in range(coast):
        lags_ref[c * SUB : (c + 1) * SUB, :] = nt(first, g_ref[c])
    size = coast * SUB
    r = iota((size, size), 0)
    q = iota((size, size), 1)
    order = ((r & (coast - 1)) == (q >> 3)) & ((r // coast) == (q & 7))
    order = order.astype(jnp.float32).astype(jnp.bfloat16)
    lags = lax.dot_general(
        order,
        lags_ref[...].astype(jnp.bfloat16),
        (((1,), (0,)), ((), ())),
        preferred_element_type=jnp.float32,
    )
    out_ref[...] = nt(lags.astype(jnp.bfloat16), pick_ref[...]).astype(jnp.bfloat16)


def shore_kernel(members, rec_ref, gp_ref, prior_ref, out_ref):
    lon_count = rec_ref.shape[0]
    coast = out_ref.shape[1]
    per = LANES // CAP
    lane = iota((SUB, LANES), 1)
    series = []
    for m in range(members):
        row = []
        for tile in range(lon_count // per):
            acc = jnp.zeros((SUB, LANES), jnp.float32)
            for j in range(per):
                v = pltpu.roll(rec_ref[tile * per + j], ((j - m) * CAP) % LANES, axis=1)
                acc = jnp.where((lane >= j * CAP) & (lane < (j + 1) * CAP), v, acc)
            row.append(acc)
        series.append(jnp.concatenate(row, axis=1))
    x = jnp.concatenate(series, axis=0)
    hi = x.astype(jnp.bfloat16)
    rest = x - hi.astype(jnp.float32)
    mid = rest.astype(jnp.bfloat16)
    lo = (rest - mid.astype(jnp.float32)).astype(jnp.bfloat16)
    r = nt(jnp.concatenate([hi, mid, lo], axis=0), gp_ref[...])
    n = members * STEPS
    r = r[0:n] + r[n : 2 * n] + r[2 * n : 3 * n]
    row8 = iota((SUB, LANES), 0)
    per = LANES // coast
    for m in range(members):
        total = jnp.zeros((SUB, LANES), jnp.float32)
        for l in range(STEPS):
            v = r[m * SUB : (m + 1) * SUB, (l // per) * LANES : (l // per + 1) * LANES]
            if l % per:
                v = pltpu.roll(v, LANES - (l % per) * coast, axis=1)
            if l:
                v = jnp.where(row8 >= l, pltpu.roll(v, l, axis=0), 0.0)
            total = total + v
        out_ref[m * SUB : (m + 1) * SUB, :] = prior_ref[m * SUB : (m + 1) * SUB, :] + total[:, 0:coast]


def local(eta_init, depth, sea_mask, probe_cells, elapsed_record, gauge_kernels):
    members, lat_cells, lon_cells = eta_init.shape
    lat_count = lax.axis_size("lat")
    lon_count = lax.axis_size("lon")
    coast, probes, lag_count = gauge_kernels.shape[1:]
    total_lat = lat_cells * lat_count
    total_lon = lon_cells * lon_count
    spacing = 2.0 * math.pi / total_lon
    courant = courant_for(total_lat, spacing)
    tiles = lon_cells // LANES
    total = lat_cells + 2 * HALO
    stride = total * tiles + total + SUB
    slots = lon_count * CAP
    f32 = jnp.float32
    vmem = pl.BlockSpec(memory_space=pltpu.VMEM)
    smem = pl.BlockSpec(memory_space=pltpu.SMEM)
    hbm = pl.BlockSpec(memory_space=pltpu.HBM)
    dma = pltpu.SemaphoreType.DMA

    def limit(mib):
        return pltpu.CompilerParams(vmem_limit_bytes=mib * MIB)

    def cost(us):
        return pl.CostEstimate(flops=0, bytes_accessed=int(us * 3.0e6), transcendentals=0)

    def stay(*arrays):
        return [pltpu.with_memory_space_constraint(a, pltpu.HBM) for a in arrays]

    halo_shape = jax.ShapeDtypeStruct(((members + 1) * HALO * tiles, LANES), f32)
    first_rows, last_rows = pl.pallas_call(
        functools.partial(rows_kernel, members),
        out_shape=[halo_shape] * 2,
        in_specs=[hbm] * 3,
        out_specs=[vmem] * 2,
        scratch_shapes=[
            pltpu.VMEM((2, members, HALO, lon_cells), f32),
            pltpu.VMEM((2, HALO, lon_cells), f32),
            pltpu.VMEM((2, HALO, lon_cells), jnp.int32),
            dma((2, 3)),
        ],
        compiler_params=limit(8),
        cost_estimate=cost(1),
        name="rows",
    )(*stay(eta_init, depth, sea_mask))
    up = [(i, i + 1) for i in range(lat_count - 1)]
    down = [(i + 1, i) for i in range(lat_count - 1)]
    top = lax.ppermute(last_rows, "lat", up)
    bottom = lax.ppermute(first_rows, "lat", down)

    first_row = lax.axis_index("lat") * lat_cells - HALO
    ids = (first_row + jnp.arange(total, dtype=jnp.int32)).astype(f32)
    latitude = -0.5 * total_lat * spacing + (ids + 0.5) * spacing
    scale = courant / jnp.cos(latitude)
    factors = jnp.stack([scale * scale, courant * jnp.cos(latitude + 0.5 * spacing), scale])
    factors = jnp.broadcast_to(factors[:, :, None], (3, total, LANES)).reshape(3 * total, LANES)

    strip = jax.ShapeDtypeStruct((DEEP * SUB, LANES), f32)
    sent, one, two, own, pick = pl.pallas_call(
        functools.partial(table_kernel, lat_cells, lon_cells, lat_count, lon_count, members),
        out_shape=[
            jax.ShapeDtypeStruct((lon_count, 1, LANES), jnp.int32),
            strip,
            strip,
            jax.ShapeDtypeStruct(((members + 1) * total, LANES), f32),
            jax.ShapeDtypeStruct((slots, probes), jnp.bfloat16),
        ],
        in_specs=[vmem, hbm, hbm, hbm],
        out_specs=[vmem] * 5,
        scratch_shapes=[
            pltpu.VMEM((2, members, lat_cells, LANES), f32),
            pltpu.VMEM((2, lat_cells, LANES), f32),
            pltpu.VMEM((2, lat_cells, LANES), jnp.int32),
            dma((2, 3)),
        ],
        compiler_params=limit(8),
        cost_estimate=cost(1.5),
        name="table",
    )(probe_cells[0], *stay(eta_init, depth, sea_mask))
    incoming = lax.all_to_all(sent, "lon", split_axis=0, concat_axis=0, tiled=True)

    recent = pl.pallas_call(
        recent_kernel,
        grid=(1,),
        out_shape=jax.ShapeDtypeStruct((STEPS * coast, slots), jnp.bfloat16),
        in_specs=[
            pl.BlockSpec((None, coast, probes, LANES), lambda k: (0, 0, 0, 0)),
            pl.BlockSpec((slots, probes), lambda k: (0, 0)),
        ],
        out_specs=pl.BlockSpec((STEPS * coast, slots), lambda k: (0, 0)),
        scratch_shapes=[pltpu.VMEM((STEPS * coast, probes), f32)],
        compiler_params=limit(12),
        cost_estimate=cost(2.5),
        name="recent",
    )(*stay(gauge_kernels), pick)

    odd = lax.rem(lax.axis_index("lon"), 2).astype(jnp.int32)[None]
    send_a, send_b = pl.pallas_call(
        functools.partial(rim_kernel, members),
        out_shape=[strip] * 2,
        in_specs=[smem] + [vmem] * 4,
        out_specs=[vmem] * 2,
        compiler_params=limit(8),
        cost_estimate=cost(0.5),
        name="rim",
    )(odd, one, two, top, bottom)
    swap_a = [(i, i ^ 1) for i in range(lon_count)]
    swap_b = [((i + 1) % lon_count, ((i ^ 1) + 1) % lon_count) for i in range(lon_count)]
    rim_a = lax.ppermute(send_a, "lon", swap_a)
    rim_b = lax.ppermute(send_b, "lon", swap_b)

    field = pltpu.VMEM((total * tiles, LANES), f32)
    tall = pltpu.VMEM((total + SUB, LANES), f32)
    eta_final, samples = pl.pallas_call(
        functools.partial(wave_kernel, members, stride),
        out_shape=[
            jax.ShapeDtypeStruct(eta_init.shape, f32),
            jax.ShapeDtypeStruct((lon_count, SUB, LANES), f32),
        ],
        in_specs=[smem] * 2 + [hbm] * 3 + [vmem] * 6,
        out_specs=[hbm, vmem],
        scratch_shapes=[
            pltpu.VMEM((members * tiles * PITCH, LANES), f32),
            pltpu.VMEM((tiles * PITCH, LANES), f32),
            pltpu.VMEM((tiles * PITCH, LANES), jnp.int32),
            field,
            field,
            field,
            tall,
            tall,
            tall,
            pltpu.VMEM(eta_init.shape, f32),
            dma(((members + 2) * tiles,)),
            dma((members,)),
        ]
        + [pltpu.VMEM(((STEPS + 1) * stride, LANES), f32)] * members
        + [field] * (2 * members)
        + [tall] * (2 * members),
        compiler_params=limit(32),
        cost_estimate=cost(11),
        name="wave",
    )(odd, incoming, *stay(eta_init, depth, sea_mask), top, bottom, rim_a, rim_b, own, factors)

    answered = lax.all_to_all(samples, "lon", split_axis=0, concat_axis=0, tiled=True)
    prior = pl.pallas_call(
        functools.partial(past_kernel, members),
        out_shape=jax.ShapeDtypeStruct((members * STEPS, coast), f32),
        in_specs=[hbm, hbm],
        out_specs=vmem,
        scratch_shapes=[
            pltpu.VMEM((probes // KTILE, coast, KTILE, lag_count), jnp.bfloat16),
            pltpu.VMEM((members, probes, lag_count), jnp.bfloat16),
            dma((probes // KTILE + 1,)),
        ],
        compiler_params=limit(28),
        cost_estimate=cost(6),
        name="past",
    )(*stay(gauge_kernels, elapsed_record))
    shore = pl.pallas_call(
        functools.partial(shore_kernel, members),
        out_shape=jax.ShapeDtypeStruct((members * STEPS, coast), f32),
        in_specs=[vmem, vmem, vmem],
        out_specs=vmem,
        compiler_params=limit(8),
        cost_estimate=cost(1),
        name="shore",
    )(answered, recent, prior)
    return eta_final, shore.reshape(1, members, STEPS, coast)


def solution(mesh):
    in_specs = (
        P(None, "lat", "lon"),
        P("lat", "lon"),
        P("lat", "lon"),
        P(("lon", "lat"), None, None),
        P(("lon", "lat"), None, None, None),
        P(("lon", "lat"), None, None, None),
    )
    out_specs = (P(None, "lat", "lon"), P(("lon", "lat"), None, None, None))
    return jax.shard_map(local, mesh=mesh, in_specs=in_specs, out_specs=out_specs, check_vma=False)
```

profile of v0, /device:TPU:11, one launch (start us, length us, event | category | flops | bytes accessed | tf_op | source)
XLA Modules:
  0.0 47.6 jit_solution(9576165282274307266)
XLA Ops:
  0.6 1.0 %rows.1 = (f32[192,128]{1,0:T(8,128)S(1)}, f32[192,128]{1,0:T(8,128)S(1)}) custom-call(f32[2,128,1024]{2,1,0:T(8,128)} %eta_ref.5, f32[128,1024]{1,0:T(8,128)} %dep_ref.5, s32[128,1024]{1,0:T(8,128)} %sea_ref.5), custom_call_target="tpu_custom_call" | custom-call | bytes 3000000 | tf_op jit(solution)/shard_map/rows/pallas_call | solution.py:517
  1.6 3.2 %collective-permute-start = (f32[192,128]{1,0:T(8,128)S(1)}, f32[192,128]{1,0:T(8,128)S(1)}, u32[]{:S(2)}, u32[]{:S(2)}) collective-permute-start(f32[192,128]{1,0:T(8,128)S(1)} %get-tuple-element.14), channel_id=1, source_target_pairs={{0,1},{1,2},{2,3},{4,5},{5,6},{6,7},{8,9},{9,10},{10,11},{12,13},{... | collective-permute-start | bytes 294920 | tf_op jit(solution)/shard_map/ppermute | solution.py:534
  4.9 2.1 %collective-permute-start.1 = (f32[192,128]{1,0:T(8,128)S(1)}, f32[192,128]{1,0:T(8,128)S(1)}, u32[]{:S(2)}, u32[]{:S(2)}) collective-permute-start(f32[192,128]{1,0:T(8,128)S(1)} %get-tuple-element.15), channel_id=1, source_target_pairs={{1,0},{2,1},{3,2},{5,4},{6,5},{7,6},{9,8},{10,9},{11,10},{13,12},{... | collective-permute-start | bytes 294920 | tf_op jit(solution)/shard_map/ppermute | solution.py:535
  6.9 0.0 copy-start
  7.0 0.7 %copy-done = s32[1,2,192]{2,1,0:T(2,128)S(1)} copy-done((s32[1,2,192]{2,1,0:T(2,128)S(1)}, s32[1,2,192]{2,1,0:T(2,128)}, u32[]{:S(2)}) %copy-start) | copy-done | bytes 1560
  7.6 1.9 %table.1 = (s32[8,1,128]{2,1,0:T(1,128)}, f32[40,128]{1,0:T(8,128)S(1)}, f32[40,128]{1,0:T(8,128)S(1)}, f32[432,128]{1,0:T(8,128)S(1)}, bf16[256,192]{1,0:T(8,128)(2,1)S(1)}) custom-call(s32[2,192]{1,0:T(2,128)S(1)} %bitcast.3, f32[2,128,1024]{2,1,0:T(8,128)} %eta_ref.5, f32[128,1024]{1,0:T(8,128)} %dep_ref.5, s32[128,1024]{1,0:T(8,128)} %sea_ref.5), custom_call_target="tpu_custom_call" | custom-call | bytes 4500000 | tf_op jit(solution)/shard_map/table/pallas_call | solution.py:545
  9.5 5.1 %all-to-all-start = ((s32[8,1,128]{2,1,0:T(1,128)}), s32[8,1,128]{2,1,0:T(1,128)S(1)}, u32[]{:S(2)}, u32[]{:S(2)}) async-start(s32[8,1,128]{2,1,0:T(1,128)} %get-tuple-element.13), calls=%async_computation | async-start | bytes 8192 | tf_op jit(solution)/shard_map/all_to_all | solution.py:566
  14.6 0.1 cosine_multiply_fusion
  14.7 0.1 fusion
  14.8 0.0 collective-permute-done.top_ref
  14.8 0.0 collective-permute-done.1.bot_ref
  14.8 0.1 rim.1
  14.9 0.4 collective-permute-start.2
  15.3 1.2 %collective-permute-start.3 = (f32[40,128]{1,0:T(8,128)S(1)}, f32[40,128]{1,0:T(8,128)S(1)}, u32[]{:S(2)}, u32[]{:S(2)}) collective-permute-start(f32[40,128]{1,0:T(8,128)S(1)} %get-tuple-element.19), channel_id=1, source_target_pairs={{4,8},{8,4},{12,16},{16,12},{20,24},{24,20},{28,0},{0,28},{5,9},{9... | collective-permute-start | bytes 61448 | tf_op jit(solution)/shard_map/ppermute | solution.py:596
  16.6 0.1 broadcast_in_dim.12
  16.6 0.8 %all-to-all-done.idx_ref = s32[8,1,128]{2,1,0:T(1,128)S(1)} async-done(((s32[8,1,128]{2,1,0:T(1,128)}), s32[8,1,128]{2,1,0:T(1,128)S(1)}, u32[]{:S(2)}, u32[]{:S(2)}) %all-to-all-start) | async-done | bytes 4128 | tf_op jit(solution)/shard_map/all_to_all | solution.py:566
  17.4 0.0 collective-permute-done.2.a_ref
  17.4 2.0 %collective-permute-done.3.b_ref = f32[40,128]{1,0:T(8,128)S(1)} collective-permute-done((f32[40,128]{1,0:T(8,128)S(1)}, f32[40,128]{1,0:T(8,128)S(1)}, u32[]{:S(2)}, u32[]{:S(2)}) %collective-permute-start.3) | collective-permute-done | bytes 20512 | tf_op jit(solution)/shard_map/ppermute | solution.py:596
  19.4 0.1 broadcast_in_dim.13.fac_ref
  19.6 11.0 %wave.1 = (f32[2,128,1024]{2,1,0:T(8,128)}, f32[8,8,128]{2,1,0:T(8,128)}) custom-call(s32[1]{0:T(128)} %bitcast.odd_ref, s32[8,1,128]{2,1,0:T(1,128)S(1)} %all-to-all-done.idx_ref, f32[2,128,1024]{2,1,0:T(8,128)} %eta_ref.5, f32[128,1024]{1,0:T(8,128)} %dep_ref.5, s32[128,1024]{1,0:T(8,128)} %sea_ref.5, f32[192,128]{1,0:T(8,128)S(1)} %collective-permute-done.top_ref, ...), custom_call_target="tpu_custom_call" | custom-call | bytes 33000000 | tf_op jit(solution)/shard_map/wave/pallas_call | solution.py:600
  30.6 4.0 %all-to-all-start.1 = ((f32[8,8,128]{2,1,0:T(8,128)}), f32[8,8,128]{2,1,0:T(8,128)S(1)}, u32[]{:S(2)}, u32[]{:S(2)}) async-start(f32[8,8,128]{2,1,0:T(8,128)} %get-tuple-element.22), calls=%async_computation.1 | async-start | bytes 65536 | tf_op jit(solution)/shard_map/all_to_all | solution.py:630
  34.5 2.6 %recent.1.gp_ref = bf16[256,256]{1,0:T(8,128)(2,1)S(1)} custom-call(bf16[1,32,192,1024]{3,2,1,0:T(8,128)(2,1)} %g_ref.3, bf16[256,192]{1,0:T(8,128)(2,1)S(1)} %get-tuple-element.23.pick_ref), custom_call_target="tpu_custom_call" | custom-call | bytes 7500000 | tf_op jit(solution)/shard_map/recent/pallas_call | solution.py:568
  37.2 9.5 %past.1.prior_ref = f32[16,32]{1,0:T(8,128)S(1)} custom-call(bf16[1,32,192,1024]{3,2,1,0:T(8,128)(2,1)} %g_ref.3, bf16[1,2,192,1024]{3,2,1,0:T(8,128)(2,1)} %e_ref.1), custom_call_target="tpu_custom_call" | custom-call | bytes 18000000 | tf_op jit(solution)/shard_map/past/pallas_call | solution.py:631
  46.7 0.0 all-to-all-done.1.rec_ref
  46.7 0.9 %shore.1 = f32[16,32]{1,0:T(8,128)} custom-call(f32[8,8,128]{2,1,0:T(8,128)S(1)} %all-to-all-done.1.rec_ref, bf16[256,256]{1,0:T(8,128)(2,1)S(1)} %recent.1.gp_ref, f32[16,32]{1,0:T(8,128)S(1)} %past.1.prior_ref), custom_call_target="tpu_custom_call" | custom-call | bytes 3000000 | tf_op jit(solution)/shard_map/shore/pallas_call | solution.py:645
  (1 shorter events, 0.0 us)
Async XLA Ops:
  1.6 13.2 %collective-permute-start = (f32[192,128]{1,0:T(8,128)S(1)}, f32[192,128]{1,0:T(8,128)S(1)}, u32[]{:S(2)}, u32[]{:S(2)}) collective-permute-start(f32[192,128]{1,0:T(8,128)S(1)} %get-tuple-element.14), channel_id=1, source_target_pairs={{0,1},{1,2},{2,3},{4,5},{5,6},{6,7},{8,9},{9,10},{10,11},{12,13},{... | collective-permute-start | bytes 294920 | tf_op jit(solution)/shard_map/ppermute | solution.py:534
  4.9 10.0 %collective-permute-start.1 = (f32[192,128]{1,0:T(8,128)S(1)}, f32[192,128]{1,0:T(8,128)S(1)}, u32[]{:S(2)}, u32[]{:S(2)}) collective-permute-start(f32[192,128]{1,0:T(8,128)S(1)} %get-tuple-element.15), channel_id=1, source_target_pairs={{1,0},{2,1},{3,2},{5,4},{6,5},{7,6},{9,8},{10,9},{11,10},{13,12},{... | collective-permute-start | bytes 294920 | tf_op jit(solution)/shard_map/ppermute | solution.py:535
  6.9 0.7 %copy-start = (s32[1,2,192]{2,1,0:T(2,128)S(1)}, s32[1,2,192]{2,1,0:T(2,128)}, u32[]{:S(2)}) copy-start(s32[1,2,192]{2,1,0:T(2,128)} %param.9) | copy-start | bytes 4612
  9.5 7.9 %all-to-all-start = ((s32[8,1,128]{2,1,0:T(1,128)}), s32[8,1,128]{2,1,0:T(1,128)S(1)}, u32[]{:S(2)}, u32[]{:S(2)}) async-start(s32[8,1,128]{2,1,0:T(1,128)} %get-tuple-element.13), calls=%async_computation | async-start | bytes 8192 | tf_op jit(solution)/shard_map/all_to_all | solution.py:566
  14.9 2.5 %collective-permute-start.2 = (f32[40,128]{1,0:T(8,128)S(1)}, f32[40,128]{1,0:T(8,128)S(1)}, u32[]{:S(2)}, u32[]{:S(2)}) collective-permute-start(f32[40,128]{1,0:T(8,128)S(1)} %get-tuple-element.18), channel_id=1, source_target_pairs={{0,4},{4,0},{8,12},{12,8},{16,20},{20,16},{24,28},{28,24},{1,5},{5... | collective-permute-start | bytes 61448 | tf_op jit(solution)/shard_map/ppermute | solution.py:595
  15.3 4.1 %collective-permute-start.3 = (f32[40,128]{1,0:T(8,128)S(1)}, f32[40,128]{1,0:T(8,128)S(1)}, u32[]{:S(2)}, u32[]{:S(2)}) collective-permute-start(f32[40,128]{1,0:T(8,128)S(1)} %get-tuple-element.19), channel_id=1, source_target_pairs={{4,8},{8,4},{12,16},{16,12},{20,24},{24,20},{28,0},{0,28},{5,9},{9... | collective-permute-start | bytes 61448 | tf_op jit(solution)/shard_map/ppermute | solution.py:596
  30.6 16.2 %all-to-all-start.1 = ((f32[8,8,128]{2,1,0:T(8,128)}), f32[8,8,128]{2,1,0:T(8,128)S(1)}, u32[]{:S(2)}, u32[]{:S(2)}) async-start(f32[8,8,128]{2,1,0:T(8,128)} %get-tuple-element.22), calls=%async_computation.1 | async-start | bytes 65536 | tf_op jit(solution)/shard_map/all_to_all | solution.py:630
where the time goes:
time: 48.1 us; the launch traced here: 47.6 us
  Pallas kernels  27 us (56%)
  starting transfers between devices  16 us (33%)
  waiting for transfers between devices  2.8 us (6%)
  local copies, waits for them, and re-layouts  0.87 us (2%)
  between operations  0.74 us (2%)
    pallas_call x1, Pallas kernels, local(): pl.pallas_call(functools.partial(wave_kernel, members, stride), out_shape...  11 us
    pallas_call x1, Pallas kernels, local(): pl.pallas_call(functools.partial(past_kernel, members), out_shape=jax.Sha...  9.53 us
    all_to_all x1, starting transfers between devices, local(): lax.all_to_all(sent, 'lon', split_axis=0, concat_axis=0, tiled=True)  5.14 us
    all_to_all x1, starting transfers between devices, local(): lax.all_to_all(samples, 'lon', split_axis=0, concat_axis=0, tiled=True)  3.97 us
    ppermute x1, starting transfers between devices, local(): top = lax.ppermute(last_rows, 'lat', up)  3.2 us
    pallas_call x1, Pallas kernels, local(): pl.pallas_call(recent_kernel, grid=(1,), out_shape=jax.ShapeDtypeStruct((...  2.64 us
    ppermute x1, starting transfers between devices, local(): bottom = lax.ppermute(first_rows, 'lat', down)  2.08 us
    ppermute x1, waiting for transfers between devices, local(): rim_b = lax.ppermute(send_b, 'lon', swap_b)  2.01 us
  transfers between devices with their start and end apart: 6, of which 2 were waited for; matrix products, arithmetic and copies ran while one was open for 0% of the time, Pallas kernels for 30%

commit v1 on v0

--- a/solution.py
+++ b/solution.py
@@ -16,7 +16,7 @@
 KTILE = 16
 GROUP = 32
 DEEP = 5
-PITCH = 136
+PARTS = 4
 MIB = 1024 * 1024
 
 
@@ -79,9 +79,11 @@
 
 def table_kernel(
     lat_cells, lon_cells, lat_count, lon_count, members,
-    cells_ref, eta_ref, dep_ref, sea_ref, msg_ref, one_ref, two_ref, own_ref, pick_ref, eta, dep, sea, sems,
+    cells_ref, eta_ref, dep_ref, sea_ref, msg_ref, one_ref, two_ref, own_ref, pick_ref, eta, dep, sea, cells, sems, cell_sem,
 ):
     tiles = lon_cells // LANES
+    table = pltpu.make_async_copy(cells_ref.at[0], cells, cell_sem.at[0])
+    table.start()
     copies = []
     for side, col in ((0, 0), (1, lon_cells - LANES)):
         for k, (src, dst) in enumerate(
@@ -95,9 +97,10 @@
             copy.start()
             copies.append(copy)
 
-    probes = cells_ref.shape[1]
-    rows = cells_ref[0:1, :]
-    cols = cells_ref[1:2, :]
+    probes = cells.shape[1]
+    table.wait()
+    rows = cells[0:1, :]
+    cols = cells[1:2, :]
     for band in range(lat_count - 1, 0, -1):
         rows = rows - jnp.where(rows >= band * lat_cells, lat_cells, 0)
     sector = jnp.zeros_like(cols)
@@ -170,7 +173,7 @@
 def rim_kernel(members, odd_ref, one_ref, two_ref, top_ref, bot_ref, a_ref, b_ref):
     tiles = top_ref.shape[0] // ((members + 1) * HALO)
     lane = iota((SUB, LANES), 1)
-    odd = odd_ref[0] == 1
+    odd = jnp.broadcast_to(odd_ref[...], (SUB, LANES)) == 1
     one = [one_ref[d * SUB : (d + 1) * SUB, :] for d in range(DEEP)]
     two = [two_ref[d * SUB : (d + 1) * SUB, :] for d in range(DEEP)]
     for ref, block in ((top_ref, 0), (bot_ref, DEEP * (LANES // GROUP) - 3)):
@@ -189,14 +192,13 @@
 
 
 def wave_kernel(
-    members, stride, odd_ref, idx_ref, eta_ref, dep_ref, sea_ref, top_ref, bot_ref, a_ref, b_ref, own_ref, fac_ref,
-    out_ref, smp_ref, eta, dep, sea, wet, ce, cn, rim_wet, rim_ce, rim_cn, out, sems, out_sems, *rest,
+    members, stride, odd_ref, idx_ref, _, pick_ref, eta_ref, dep_ref, sea_ref, g_ref, top_ref, bot_ref, a_ref, b_ref, own_ref, fac_ref,
+    out_ref, smp_ref, gp_ref, eta, dep, sea, wet, ce, cw, cn, rim_wet, rim_ce, rim_cn, out, places, taps, lags, sems, out_sems, idx_sem, *rest,
 ):
     hist = rest[:members]
-    east = rest[members : 2 * members]
-    north = rest[2 * members : 3 * members]
-    rim_east = rest[3 * members : 4 * members]
-    rim_north = rest[4 * members : 5 * members]
+    past = rest[members : 2 * members]
+    rim_east = rest[2 * members : 3 * members]
+    rim_north = rest[3 * members : 4 * members]
     rows = eta_ref.shape[1]
     tiles = eta_ref.shape[2] // LANES
     total = rows + 2 * HALO
@@ -206,19 +208,27 @@
     row8 = iota((SUB, LANES), 0)
     last = lane == LANES - 1
     first = lane == 0
-    odd = odd_ref[0] == 1
+    odd = jnp.broadcast_to(odd_ref[...], (SUB, LANES)) == 1
     zero = jnp.zeros((SUB, LANES), jnp.float32)
 
-    copies = []
-    for t in range(tiles):
-        cols = pl.ds(t * LANES, LANES)
-        for m in range(members):
-            copies.append((eta_ref.at[m, :, cols], eta.at[pl.ds((m * tiles + t) * PITCH, rows), :]))
-        copies.append((dep_ref.at[:, cols], dep.at[pl.ds(t * PITCH, rows), :]))
-        copies.append((sea_ref.at[:, cols], sea.at[pl.ds(t * PITCH, rows), :]))
-    copies = [pltpu.make_async_copy(a, b, sems.at[k]) for k, (a, b) in enumerate(copies)]
-    for copy in copies:
-        copy.start()
+    part = rows // PARTS
+    arriving = []
+    for k in range(PARTS):
+        at = pl.ds(k * part, part)
+        arriving.append(
+            [
+                pltpu.make_async_copy(eta_ref.at[:, at, :], eta.at[:, at, :], sems.at[k, 0]),
+                pltpu.make_async_copy(dep_ref.at[at, :], dep.at[at, :], sems.at[k, 1]),
+                pltpu.make_async_copy(sea_ref.at[at, :], sea.at[at, :], sems.at[k, 2]),
+            ]
+        )
+        for copy in arriving[k]:
+            copy.start()
+    to_scalar = pltpu.make_async_copy(idx_ref, places, idx_sem.at[0])
+    to_scalar.start()
+    tapped = pltpu.make_async_copy(g_ref.at[0, :, :, pl.ds(0, LANES)], taps, idx_sem.at[1])
+    tapped.start()
+    coast = taps.shape[0]
 
     def shl(v):
         v = pltpu.roll(v, LANES - 1, axis=1)
@@ -278,32 +288,87 @@
         for m in range(members):
             hist[m][row * tiles : row * tiles + size, :] = ref[m * size : (m + 1) * size, :]
         wet[row * tiles : row * tiles + size, :] = ref[members * size : (members + 1) * size, :]
-    for copy in copies:
-        copy.wait()
-    for r in range(rows):
-        here = sea[pl.ds(r, tiles, stride=PITCH), :].astype(jnp.float32)
+    done = 0
+    for k in range(PARTS):
+        for copy in arriving[k]:
+            copy.wait()
+        for b in range(k * part // SUB, (k + 1) * part // SUB):
+            for t in range(tiles):
+                cols = slice(t * LANES, (t + 1) * LANES)
+                at = pl.ds((HALO + b * SUB) * tiles + t, SUB, stride=tiles)
+                here = sea[blk(b), cols].astype(jnp.float32)
+                for m in range(members):
+                    hist[m][at, :] = eta[m, blk(b), cols] * here
+                wet[at, :] = dep[blk(b), cols] * here
+        ready = total - 1 if k == PARTS - 1 else HALO + (k + 1) * part - 1
+        w = wet[vec(done), :]
+        for r in range(done, ready):
+            below = wet[vec(r + 1), :]
+            edge = fac(0, r) * jnp.sqrt(w * shl(w))
+            ce[vec(r), :] = edge
+            cw[vec(r), :] = shr(edge)
+            cn[vec(r), :] = fac(1, r) * jnp.sqrt(w * below)
+            w = below
+        done = ready
+
+    leaving = []
+    end = STEPS * stride
+
+    def finish(b):
         for m in range(members):
-            hist[m][vec(r + HALO), :] = eta[pl.ds(m * tiles * PITCH + r, tiles, stride=PITCH), :] * here
-        wet[vec(r + HALO), :] = dep[pl.ds(r, tiles, stride=PITCH), :] * here
-    w = wet[vec(0), :]
-    for r in range(total - 1):
-        below = wet[vec(r + 1), :]
-        ce[vec(r), :] = fac(0, r) * jnp.sqrt(w * shl(w))
-        cn[vec(r), :] = fac(1, r) * jnp.sqrt(w * below)
-        w = below
+            at = end + rim + HALO + b * SUB
+            edge = hist[m][at : at + SUB, :]
+            for t in range(tiles):
+                v = hist[m][pl.ds(end + (HALO + b * SUB) * tiles + t, SUB, stride=tiles), :]
+                if t == 0:
+                    v = jnp.where(lane < HALO, pltpu.roll(edge, 2 * HALO, axis=1), v)
+                if t == tiles - 1:
+                    v = jnp.where(lane >= LANES - HALO, pltpu.roll(edge, LANES - 2 * HALO, axis=1), v)
+                out[m, blk(b), t * LANES : (t + 1) * LANES] = v
+        if (b + 1) * SUB % part == 0:
+            k = (b + 1) * SUB // part - 1
+            at = pl.ds(k * part, part)
+            copy = pltpu.make_async_copy(out.at[:, at, :], out_ref.at[:, at, :], out_sems.at[k])
+            copy.start()
+            leaving.append(copy)
+
+    def read_taps(c):
+        unit = (iota((SUB, LANES), 0) == iota((SUB, LANES), 1)).astype(jnp.float32).astype(jnp.bfloat16)
+        lags[c * SUB : (c + 1) * SUB, :] = nt(unit, taps[c])
+
+    def sort_taps():
+        size = coast * SUB
+        r = iota((size, size), 0)
+        c = iota((size, size), 1)
+        order = ((r & (coast - 1)) == (c >> 3)) & ((r // coast) == (c & 7))
+        ordered = lax.dot_general(
+            order.astype(jnp.float32).astype(jnp.bfloat16),
+            lags[...].astype(jnp.bfloat16),
+            (((1,), (0,)), ((), ())),
+            preferred_element_type=jnp.float32,
+        )
+        gp_ref[...] = nt(ordered.astype(jnp.bfloat16), pick_ref[...]).astype(jnp.bfloat16)
 
     for q in range(STEPS):
         low, high = q + 1, total - 1 - q
         base = q * stride
         after = base + stride
-        s, above = [], []
+        s, sums, above = [], [], []
+
+        def summed(m, r, v):
+            if q == 0:
+                return v
+            old = hist[m][vec(r), :] if q == 1 else past[m][vec(r), :]
+            new = old + v
+            if q < STEPS - 1:
+                past[m][vec(r), :] = new
+            return new
+
         for m in range(members):
-            before = hist[m][base + (low - 1) * tiles : base + low * tiles, :]
+            before = summed(m, low - 1, hist[m][base + (low - 1) * tiles : base + low * tiles, :])
             s.append(hist[m][base + low * tiles : base + (low + 1) * tiles, :])
-            n = s[m] - before
-            if q:
-                n = north[m][vec(low - 1), :] + n
-            above.append(cn[vec(low - 1), :] * n)
+            sums.append(summed(m, low, s[m]))
+            above.append(cn[vec(low - 1), :] * (sums[m] - before))
         rim_above = [zero] * members
 
         def rim_block(b):
@@ -331,50 +396,37 @@
         for r in range(low, high):
             if r % SUB == 0:
                 rim_block(r // SUB - 1)
+            if q == 2 and r % 4 == 0 and r // 4 <= coast:
+                if r == 4:
+                    tapped.wait()
+                read_taps(r // 4 - 1)
+            if q == 4 and r == rows // 2:
+                sort_taps()
             scale = fac(2, r)
             to_east = ce[vec(r), :]
+            to_west = cw[vec(r), :]
             to_north = cn[vec(r), :]
             for m in range(members):
                 below = hist[m][base + (r + 1) * tiles : base + (r + 2) * tiles, :]
-                e = shl(s[m]) - s[m]
-                n = below - s[m]
-                if q:
-                    e = east[m][vec(r), :] + e
-                    n = north[m][vec(r), :] + n
-                fe = to_east * e
-                fn = to_north * n
-                if q < STEPS - 1:
-                    east[m][vec(r), :] = e
-                    north[m][vec(r), :] = n
+                sum_below = summed(m, r + 1, below)
+                pulled = to_east * (shl(sums[m]) - sums[m]) - to_west * (sums[m] - shr(sums[m]))
+                fn = to_north * (sum_below - sums[m])
                 hist[m][after + r * tiles : after + (r + 1) * tiles, :] = s[m] + (
-                    (fe - shr(fe)) + scale * (fn - above[m])
+                    pulled + scale * (fn - above[m])
                 )
                 s[m] = below
+                sums[m] = sum_below
                 above[m] = fn
+            if q == STEPS - 1 and r % SUB == SUB - 1 and r >= HALO + 2 * SUB - 1:
+                finish((r - HALO) // SUB - 1)
         for b in range((high - 1) // SUB, blocks):
             rim_block(b)
-
-    copies = []
-    end = STEPS * stride
-    for m in range(members):
-        for b in range(rows // SUB):
-            at = end + rim + HALO + b * SUB
-            edge = hist[m][at : at + SUB, :]
-            for t in range(tiles):
-                v = hist[m][pl.ds(end + (HALO + b * SUB) * tiles + t, SUB, stride=tiles), :]
-                if t == 0:
-                    v = jnp.where(lane < HALO, pltpu.roll(edge, 2 * HALO, axis=1), v)
-                if t == tiles - 1:
-                    v = jnp.where(lane >= LANES - HALO, pltpu.roll(edge, LANES - 2 * HALO, axis=1), v)
-                out[m, blk(b), t * LANES : (t + 1) * LANES] = v
-        copy = pltpu.make_async_copy(out.at[m], out_ref.at[m], out_sems.at[m])
-        copy.start()
-        copies.append(copy)
+    finish(rows // SUB - 1)
 
     def sample(s, carry):
         acc = zero
         for j in range(CAP):
-            code = idx_ref[s, 0, j]
+            code = places[s, 0, j]
             spot = lax.bitwise_and(code, LANES - 1)
             place = lax.shift_right_logical(code, 7) + (stride + HALO * tiles)
             for m in range(members):
@@ -385,70 +437,51 @@
         smp_ref[s] = acc
         return carry
 
+    to_scalar.wait()
     lax.fori_loop(0, smp_ref.shape[0], sample, 0)
-    for copy in copies:
+    for copy in leaving:
         copy.wait()
 
 
-def past_kernel(members, g_ref, e_ref, out_ref, g, e, sems):
-    coast, probes, lag_count = g_ref.shape[1:]
-    parts = probes // KTILE
-    copies = [pltpu.make_async_copy(e_ref.at[0], e, sems.at[parts])]
-    for k in range(parts):
-        at = pl.ds(k * KTILE, KTILE)
-        copies.append(pltpu.make_async_copy(g_ref.at[0, :, at, :], g.at[k], sems.at[k]))
-    for copy in copies:
-        copy.start()
-    copies[0].wait()
+def past_kernel(members, g_ref, e_ref, _, out_ref, acc_ref):
+    coast, probes, lag_count = g_ref.shape
+    step = pl.program_id(0)
     lane = iota((members * KTILE, LANES), 1)
-
-    def windows(k):
-        past = e[:, k * KTILE : (k + 1) * KTILE, :].reshape(members * KTILE, lag_count).astype(jnp.float32)
+    rows = []
+    windows = []
+    for k in range(probes // KTILE):
+        at = slice(k * KTILE, (k + 1) * KTILE)
+        past = e_ref[:, at, :].reshape(members * KTILE, lag_count).astype(jnp.float32)
         shifted = []
         for t in range(1, STEPS + 1):
             moved = pltpu.roll(past, t, axis=1)
             start = jnp.where(lane >= t, moved[:, :LANES], 0.0)
             shifted.append(jnp.concatenate([start, moved[:, LANES:]], axis=1).astype(jnp.bfloat16))
-        return jnp.concatenate(shifted, axis=0)
-
-    acc = None
-    for k in range(0, parts, 2):
-        w = jnp.concatenate([windows(k), windows(k + 1)], axis=1)
-        copies[1 + k].wait()
-        copies[2 + k].wait()
-        x = jnp.concatenate([g[k + i].reshape(coast * KTILE, lag_count) for i in range(2)], axis=1)
-        part = nt(x, w)
-        acc = part if acc is None else acc + part
-    same = (iota(acc.shape, 0) & (KTILE - 1)) == (iota(acc.shape, 1) & (KTILE - 1))
-    kept = jnp.sum(jnp.where(same, acc, 0.0).reshape(coast, KTILE, acc.shape[1]), axis=1)
-    wins = members * STEPS
-    row = iota((wins, acc.shape[1]), 0)
-    col = iota((wins, acc.shape[1]), 1)
-    fold = ((col // KTILE) == (row & (STEPS - 1)) * members + row // STEPS).astype(jnp.float32)
-    out_ref[...] = nt(fold, kept, precision=lax.Precision.HIGHEST)
-
-
-def recent_kernel(g_ref, pick_ref, out_ref, lags_ref):
-    coast = g_ref.shape[0]
-    probes = g_ref.shape[1]
-    first = (iota((SUB, LANES), 0) == iota((SUB, LANES), 1)).astype(jnp.float32).astype(jnp.bfloat16)
-    for c in range(coast):
-        lags_ref[c * SUB : (c + 1) * SUB, :] = nt(first, g_ref[c])
-    size = coast * SUB
-    r = iota((size, size), 0)
-    q = iota((size, size), 1)
-    order = ((r & (coast - 1)) == (q >> 3)) & ((r // coast) == (q & 7))
-    order = order.astype(jnp.float32).astype(jnp.bfloat16)
-    lags = lax.dot_general(
-        order,
-        lags_ref[...].astype(jnp.bfloat16),
-        (((1,), (0,)), ((), ())),
-        preferred_element_type=jnp.float32,
-    )
-    out_ref[...] = nt(lags.astype(jnp.bfloat16), pick_ref[...]).astype(jnp.bfloat16)
-
-
-def shore_kernel(members, rec_ref, gp_ref, prior_ref, out_ref):
+        windows.append(jnp.concatenate(shifted, axis=0))
+        rows.append(g_ref[:, at, :].reshape(coast * KTILE, lag_count))
+    part = nt(jnp.concatenate(rows, axis=1), jnp.concatenate(windows, axis=1))
+
+    @pl.when(step == 0)
+    def _():
+        acc_ref[...] = part
+
+    @pl.when(step > 0)
+    def _():
+        acc_ref[...] += part
+
+    @pl.when(step == pl.num_programs(0) - 1)
+    def _():
+        acc = acc_ref[...]
+        same = (iota(acc.shape, 0) & (KTILE - 1)) == (iota(acc.shape, 1) & (KTILE - 1))
+        kept = jnp.sum(jnp.where(same, acc, 0.0).reshape(coast, KTILE, acc.shape[1]), axis=1)
+        wins = members * STEPS
+        row = iota((wins, acc.shape[1]), 0)
+        col = iota((wins, acc.shape[1]), 1)
+        fold = ((col // KTILE) == (row & (STEPS - 1)) * members + row // STEPS).astype(jnp.float32)
+        out_ref[...] = nt(fold, kept, precision=lax.Precision.HIGHEST)
+
+
+def shore_kernel(members, rec_ref, gp_ref, prior_ref, few_ref, out_ref):
     lon_count = rec_ref.shape[0]
     coast = out_ref.shape[1]
     per = LANES // CAP
@@ -482,7 +515,7 @@
             if l:
                 v = jnp.where(row8 >= l, pltpu.roll(v, l, axis=0), 0.0)
             total = total + v
-        out_ref[m * SUB : (m + 1) * SUB, :] = prior_ref[m * SUB : (m + 1) * SUB, :] + total[:, 0:coast]
+        out_ref[m * SUB : (m + 1) * SUB, :] = (prior_ref[m * SUB : (m + 1) * SUB, :] + few_ref[m * SUB : (m + 1) * SUB, :]) + total[:, 0:coast]
 
 
 def local(eta_init, depth, sea_mask, probe_cells, elapsed_record, gauge_kernels):
@@ -551,40 +584,27 @@
             jax.ShapeDtypeStruct(((members + 1) * total, LANES), f32),
             jax.ShapeDtypeStruct((slots, probes), jnp.bfloat16),
         ],
-        in_specs=[vmem, hbm, hbm, hbm],
+        in_specs=[hbm] * 4,
         out_specs=[vmem] * 5,
         scratch_shapes=[
             pltpu.VMEM((2, members, lat_cells, LANES), f32),
             pltpu.VMEM((2, lat_cells, LANES), f32),
             pltpu.VMEM((2, lat_cells, LANES), jnp.int32),
+            pltpu.VMEM(probe_cells.shape[1:], jnp.int32),
             dma((2, 3)),
+            dma((1,)),
         ],
         compiler_params=limit(8),
         cost_estimate=cost(1.5),
         name="table",
-    )(probe_cells[0], *stay(eta_init, depth, sea_mask))
+    )(*stay(probe_cells, eta_init, depth, sea_mask))
     incoming = lax.all_to_all(sent, "lon", split_axis=0, concat_axis=0, tiled=True)
 
-    recent = pl.pallas_call(
-        recent_kernel,
-        grid=(1,),
-        out_shape=jax.ShapeDtypeStruct((STEPS * coast, slots), jnp.bfloat16),
-        in_specs=[
-            pl.BlockSpec((None, coast, probes, LANES), lambda k: (0, 0, 0, 0)),
-            pl.BlockSpec((slots, probes), lambda k: (0, 0)),
-        ],
-        out_specs=pl.BlockSpec((STEPS * coast, slots), lambda k: (0, 0)),
-        scratch_shapes=[pltpu.VMEM((STEPS * coast, probes), f32)],
-        compiler_params=limit(12),
-        cost_estimate=cost(2.5),
-        name="recent",
-    )(*stay(gauge_kernels), pick)
-
-    odd = lax.rem(lax.axis_index("lon"), 2).astype(jnp.int32)[None]
+    odd = jnp.broadcast_to(lax.rem(lax.axis_index("lon"), 2).astype(jnp.int32), (1, LANES))
     send_a, send_b = pl.pallas_call(
         functools.partial(rim_kernel, members),
         out_shape=[strip] * 2,
-        in_specs=[smem] + [vmem] * 4,
+        in_specs=[vmem] * 5,
         out_specs=[vmem] * 2,
         compiler_params=limit(8),
         cost_estimate=cost(0.5),
@@ -595,20 +615,44 @@
     rim_a = lax.ppermute(send_a, "lon", swap_a)
     rim_b = lax.ppermute(send_b, "lon", swap_b)
 
+    few = 2 * KTILE
+    half = (probes - few) // 2
+
+    def past_sum(size, first, count, after, name, us):
+        return pl.pallas_call(
+            functools.partial(past_kernel, members),
+            grid=(count,),
+            out_shape=jax.ShapeDtypeStruct((members * STEPS, coast), f32),
+            in_specs=[
+                pl.BlockSpec((None, coast, size, lag_count), lambda k: (0, 0, k + first, 0)),
+                pl.BlockSpec((None, members, size, lag_count), lambda k: (0, 0, k + first, 0)),
+                pl.BlockSpec((SUB, LANES), lambda k: (0, 0)),
+            ],
+            out_specs=pl.BlockSpec((members * STEPS, coast), lambda k: (0, 0)),
+            scratch_shapes=[pltpu.VMEM((coast * KTILE, members * STEPS * KTILE), f32)],
+            compiler_params=limit(26),
+            cost_estimate=cost(us),
+            name=name,
+        )(*stay(gauge_kernels, elapsed_record), after)
+
+    prior_few = past_sum(few, (probes - few) // few, 1, send_a, "past_few", 1.5)
+
     field = pltpu.VMEM((total * tiles, LANES), f32)
     tall = pltpu.VMEM((total + SUB, LANES), f32)
-    eta_final, samples = pl.pallas_call(
+    eta_final, samples, recent = pl.pallas_call(
         functools.partial(wave_kernel, members, stride),
         out_shape=[
             jax.ShapeDtypeStruct(eta_init.shape, f32),
             jax.ShapeDtypeStruct((lon_count, SUB, LANES), f32),
+            jax.ShapeDtypeStruct((STEPS * coast, slots), jnp.bfloat16),
         ],
-        in_specs=[smem] * 2 + [hbm] * 3 + [vmem] * 6,
-        out_specs=[hbm, vmem],
+        in_specs=[vmem] * 4 + [hbm] * 4 + [vmem] * 6,
+        out_specs=[hbm, vmem, vmem],
         scratch_shapes=[
-            pltpu.VMEM((members * tiles * PITCH, LANES), f32),
-            pltpu.VMEM((tiles * PITCH, LANES), f32),
-            pltpu.VMEM((tiles * PITCH, LANES), jnp.int32),
+            pltpu.VMEM(eta_init.shape, f32),
+            pltpu.VMEM(depth.shape, f32),
+            pltpu.VMEM(depth.shape, jnp.int32),
+            field,
             field,
             field,
             field,
@@ -616,41 +660,32 @@
             tall,
             tall,
             pltpu.VMEM(eta_init.shape, f32),
-            dma(((members + 2) * tiles,)),
-            dma((members,)),
+            pltpu.SMEM((lon_count, 1, LANES), jnp.int32),
+            pltpu.VMEM((coast, probes, LANES), jnp.bfloat16),
+            pltpu.VMEM((coast * SUB, probes), f32),
+            dma((PARTS, 3)),
+            dma((PARTS,)),
+            dma((2,)),
         ]
         + [pltpu.VMEM(((STEPS + 1) * stride, LANES), f32)] * members
-        + [field] * (2 * members)
+        + [field] * members
         + [tall] * (2 * members),
-        compiler_params=limit(32),
+        compiler_params=limit(36),
         cost_estimate=cost(11),
         name="wave",
-    )(odd, incoming, *stay(eta_init, depth, sea_mask), top, bottom, rim_a, rim_b, own, factors)
+    )(odd, incoming, prior_few, pick, *stay(eta_init, depth, sea_mask, gauge_kernels), top, bottom, rim_a, rim_b, own, factors)
 
     answered = lax.all_to_all(samples, "lon", split_axis=0, concat_axis=0, tiled=True)
-    prior = pl.pallas_call(
-        functools.partial(past_kernel, members),
-        out_shape=jax.ShapeDtypeStruct((members * STEPS, coast), f32),
-        in_specs=[hbm, hbm],
-        out_specs=vmem,
-        scratch_shapes=[
-            pltpu.VMEM((probes // KTILE, coast, KTILE, lag_count), jnp.bfloat16),
-            pltpu.VMEM((members, probes, lag_count), jnp.bfloat16),
-            dma((probes // KTILE + 1,)),
-        ],
-        compiler_params=limit(28),
-        cost_estimate=cost(6),
-        name="past",
-    )(*stay(gauge_kernels, elapsed_record))
+    prior = past_sum(half, 0, 2, samples.reshape(-1, LANES), "past", 6)
     shore = pl.pallas_call(
         functools.partial(shore_kernel, members),
         out_shape=jax.ShapeDtypeStruct((members * STEPS, coast), f32),
-        in_specs=[vmem, vmem, vmem],
+        in_specs=[vmem] * 4,
         out_specs=vmem,
         compiler_params=limit(8),
         cost_estimate=cost(1),
         name="shore",
-    )(answered, recent, prior)
+    )(answered, recent, prior, prior_few)
     return eta_final, shore.reshape(1, members, STEPS, coast)
 
 

time: 48.1 us -> 42 us (0.87)
  Pallas kernels: 27 us -> 24.1 us
  waiting for transfers between devices: 2.8 us -> 0.02 us
  local copies, waits for them, and re-layouts: 0.87 us -> 0.2 us
    pallas_call x2, Pallas kernels: 12.2 us -> 8.84 us  [past_sum(): pl.pallas_call(functools.partial(past_kernel, members), grid=(count,), ou...]
    ppermute x1, waiting for transfers between devices: 2.01 us -> 0.01 us  [local(): rim_b = lax.ppermute(send_b, 'lon', swap_b)]
    all_to_all x1, waiting for transfers between devices: 0.78 us -> 0.01 us  [local(): lax.all_to_all(sent, 'lon', split_axis=0, concat_axis=0, tiled=True)]
    unnamed x2 -> x0, local copies, waits for them, and re-layouts: 0.68 us -> none
    all_to_all x1, starting transfers between devices: 3.97 us -> 4.5 us  [local(): lax.all_to_all(samples, 'lon', split_axis=0, concat_axis=0, tiled=True)]
  transfers between devices with their start and end apart: 6 -> 6, of which waited for: 2 -> 0; matrix products, arithmetic and copies ran while one was open for 0% -> 1% of each run, Pallas kernels for 30% -> 26%
where the time goes in v1:
time: 42 us; the launch traced here: 41.7 us
  Pallas kernels  24.1 us (57%)
  starting transfers between devices  16.4 us (39%)
  between operations  0.75 us (2%)
    pallas_call x1, Pallas kernels, local(): pl.pallas_call(functools.partial(wave_kernel, members, stride), out_shape...  11.2 us
    pallas_call x2, Pallas kernels, past_sum(): pl.pallas_call(functools.partial(past_kernel, members), grid=(count,), ou...  8.84 us
    all_to_all x1, starting transfers between devices, local(): lax.all_to_all(sent, 'lon', split_axis=0, concat_axis=0, tiled=True)  5.14 us
    all_to_all x1, starting transfers between devices, local(): lax.all_to_all(samples, 'lon', split_axis=0, concat_axis=0, tiled=True)  4.5 us
    ppermute x1, starting transfers between devices, local(): top = lax.ppermute(last_rows, 'lat', up)  3.2 us
    pallas_call x1, Pallas kernels, local(): pl.pallas_call(functools.partial(table_kernel, lat_cells, lon_cells, lat_...  2.09 us
    ppermute x1, starting transfers between devices, local(): bottom = lax.ppermute(first_rows, 'lat', down)  2.08 us
    ppermute x1, starting transfers between devices, local(): rim_b = lax.ppermute(send_b, 'lon', swap_b)  1.5 us
  transfers between devices with their start and end apart: 6, of which 0 were waited for; matrix products, arithmetic and copies ran while one was open for 1% of the time, Pallas kernels for 26%

profile of v1, /device:TPU:11, one launch (start us, length us, event | category | flops | bytes accessed | tf_op | source)
XLA Modules:
  0.0 41.7 jit_solution(3342368668272764167)
XLA Ops:
  0.6 1.0 %rows.1 = (f32[192,128]{1,0:T(8,128)S(1)}, f32[192,128]{1,0:T(8,128)S(1)}) custom-call(f32[2,128,1024]{2,1,0:T(8,128)} %eta_ref.5, f32[128,1024]{1,0:T(8,128)} %dep_ref.5, s32[128,1024]{1,0:T(8,128)} %sea_ref.5), custom_call_target="tpu_custom_call" | custom-call | bytes 3000000 | tf_op jit(solution)/shard_map/rows/pallas_call | solution.py:550
  1.6 3.2 %collective-permute-start = (f32[192,128]{1,0:T(8,128)S(1)}, f32[192,128]{1,0:T(8,128)S(1)}, u32[]{:S(2)}, u32[]{:S(2)}) collective-permute-start(f32[192,128]{1,0:T(8,128)S(1)} %get-tuple-element.17), channel_id=1, source_target_pairs={{0,1},{1,2},{2,3},{4,5},{5,6},{6,7},{8,9},{9,10},{10,11},{12,13},{... | collective-permute-start | bytes 294920 | tf_op jit(solution)/shard_map/ppermute | solution.py:567
  4.9 2.1 %collective-permute-start.1 = (f32[192,128]{1,0:T(8,128)S(1)}, f32[192,128]{1,0:T(8,128)S(1)}, u32[]{:S(2)}, u32[]{:S(2)}) collective-permute-start(f32[192,128]{1,0:T(8,128)S(1)} %get-tuple-element.18), channel_id=1, source_target_pairs={{1,0},{2,1},{3,2},{5,4},{6,5},{7,6},{9,8},{10,9},{11,10},{13,12},{... | collective-permute-start | bytes 294920 | tf_op jit(solution)/shard_map/ppermute | solution.py:568
  6.9 2.1 %table.1 = (s32[8,1,128]{2,1,0:T(1,128)}, f32[40,128]{1,0:T(8,128)S(1)}, f32[40,128]{1,0:T(8,128)S(1)}, f32[432,128]{1,0:T(8,128)S(1)}, bf16[256,192]{1,0:T(8,128)(2,1)S(1)}) custom-call(s32[1,2,192]{2,1,0:T(2,128)} %cells_ref.1, f32[2,128,1024]{2,1,0:T(8,128)} %eta_ref.5, f32[128,1024]{1,0:T(8,128)} %dep_ref.5, s32[128,1024]{1,0:T(8,128)} %sea_ref.5), custom_call_target="tpu_custom_call" | custom-call | bytes 4500000 | tf_op jit(solution)/shard_map/table/pallas_call | solution.py:578
  9.0 5.1 %all-to-all-start = ((s32[8,1,128]{2,1,0:T(1,128)}), s32[8,1,128]{2,1,0:T(1,128)S(1)}, u32[]{:S(2)}, u32[]{:S(2)}) async-start(s32[8,1,128]{2,1,0:T(1,128)} %get-tuple-element.14), calls=%async_computation | async-start | bytes 8192 | tf_op jit(solution)/shard_map/all_to_all | solution.py:601
  14.2 0.1 cosine_multiply_fusion
  14.3 0.1 fusion
  14.3 0.0 collective-permute-done.top_ref
  14.3 0.0 collective-permute-done.1.bot_ref
  14.4 0.1 rim.1
  14.5 1.5 %collective-permute-start.3 = (f32[40,128]{1,0:T(8,128)S(1)}, f32[40,128]{1,0:T(8,128)S(1)}, u32[]{:S(2)}, u32[]{:S(2)}) collective-permute-start(f32[40,128]{1,0:T(8,128)S(1)} %get-tuple-element.21), channel_id=1, source_target_pairs={{4,8},{8,4},{12,16},{16,12},{20,24},{24,20},{28,0},{0,28},{5,9},{9... | collective-permute-start | bytes 61448 | tf_op jit(solution)/shard_map/ppermute | solution.py:616
  15.9 0.0 collective-permute-start.2
  16.0 0.1 broadcast_in_dim.12
  16.1 2.6 %past_few.1._.few_ref = f32[16,32]{1,0:T(8,128)S(1)} custom-call(bf16[1,32,192,1024]{3,2,1,0:T(8,128)(2,1)} %g_ref.5, bf16[1,2,192,1024]{3,2,1,0:T(8,128)(2,1)} %e_ref.3, f32[40,128]{1,0:T(8,128)S(1)} %get-tuple-element.19._), custom_call_target="tpu_custom_call" | custom-call | bytes 4500000 | tf_op jit(solution)/shard_map/past_few/pallas_call | solution.py:622
  18.7 0.0 all-to-all-done.idx_ref
  18.7 0.0 collective-permute-done.3.b_ref
  18.7 0.0 collective-permute-done.2.a_ref
  18.7 0.1 broadcast_in_dim.13.fac_ref
  18.8 11.2 %wave.1 = (f32[2,128,1024]{2,1,0:T(8,128)}, f32[8,8,128]{2,1,0:T(8,128)}, bf16[256,256]{1,0:T(8,128)(2,1)S(1)}) custom-call(s32[1,128]{1,0:T(1,128)S(1)} %broadcast_in_dim.11.odd_ref, s32[8,1,128]{2,1,0:T(1,128)S(1)} %all-to-all-done.idx_ref, f32[16,32]{1,0:T(8,128)S(1)} %past_few.1._.few_ref, bf16[256,192]{1,0:T(8,128)(2,1)S(1)} %get-tuple-element.20.pick_ref, ...), custom_call_target="tpu_custom_call" | custom-call | bytes 33000000 | tf_op jit(solution)/shard_map/wave/pallas_call | solution.py:642
  30.0 4.5 %all-to-all-start.1 = ((f32[8,8,128]{2,1,0:T(8,128)}), f32[8,8,128]{2,1,0:T(8,128)S(1)}, u32[]{:S(2)}, u32[]{:S(2)}) async-start(f32[8,8,128]{2,1,0:T(8,128)} %get-tuple-element.24), calls=%async_computation.1 | async-start | bytes 65536 | tf_op jit(solution)/shard_map/all_to_all | solution.py:678
  34.5 6.2 %past.1.prior_ref = f32[16,32]{1,0:T(8,128)S(1)} custom-call(bf16[1,32,192,1024]{3,2,1,0:T(8,128)(2,1)} %g_ref.5, bf16[1,2,192,1024]{3,2,1,0:T(8,128)(2,1)} %e_ref.3, f32[64,128]{1,0:T(8,128)} %bitcast._), custom_call_target="tpu_custom_call" | custom-call | bytes 18000000 | tf_op jit(solution)/shard_map/past/pallas_call | solution.py:622
  40.8 0.0 all-to-all-done.1.rec_ref
  40.8 0.9 %shore.1 = f32[16,32]{1,0:T(8,128)} custom-call(f32[8,8,128]{2,1,0:T(8,128)S(1)} %all-to-all-done.1.rec_ref, bf16[256,256]{1,0:T(8,128)(2,1)S(1)} %get-tuple-element.25.gp_ref, f32[16,32]{1,0:T(8,128)S(1)} %past.1.prior_ref, f32[16,32]{1,0:T(8,128)S(1)} %past_few.1._.few_ref), custom_call_target="tpu_custom_call" | custom-call | bytes 3000000 | tf_op jit(solution)/shard_map/shore/pallas_call | solution.py:680
  (2 shorter events, 0.0 us)
Async XLA Ops:
  1.6 12.7 %collective-permute-start = (f32[192,128]{1,0:T(8,128)S(1)}, f32[192,128]{1,0:T(8,128)S(1)}, u32[]{:S(2)}, u32[]{:S(2)}) collective-permute-start(f32[192,128]{1,0:T(8,128)S(1)} %get-tuple-element.17), channel_id=1, source_target_pairs={{0,1},{1,2},{2,3},{4,5},{5,6},{6,7},{8,9},{9,10},{10,11},{12,13},{... | collective-permute-start | bytes 294920 | tf_op jit(solution)/shard_map/ppermute | solution.py:567
  4.9 9.5 %collective-permute-start.1 = (f32[192,128]{1,0:T(8,128)S(1)}, f32[192,128]{1,0:T(8,128)S(1)}, u32[]{:S(2)}, u32[]{:S(2)}) collective-permute-start(f32[192,128]{1,0:T(8,128)S(1)} %get-tuple-element.18), channel_id=1, source_target_pairs={{1,0},{2,1},{3,2},{5,4},{6,5},{7,6},{9,8},{10,9},{11,10},{13,12},{... | collective-permute-start | bytes 294920 | tf_op jit(solution)/shard_map/ppermute | solution.py:568
  9.0 9.6 %all-to-all-start = ((s32[8,1,128]{2,1,0:T(1,128)}), s32[8,1,128]{2,1,0:T(1,128)S(1)}, u32[]{:S(2)}, u32[]{:S(2)}) async-start(s32[8,1,128]{2,1,0:T(1,128)} %get-tuple-element.14), calls=%async_computation | async-start | bytes 8192 | tf_op jit(solution)/shard_map/all_to_all | solution.py:601
  14.5 4.2 %collective-permute-start.3 = (f32[40,128]{1,0:T(8,128)S(1)}, f32[40,128]{1,0:T(8,128)S(1)}, u32[]{:S(2)}, u32[]{:S(2)}) collective-permute-start(f32[40,128]{1,0:T(8,128)S(1)} %get-tuple-element.21), channel_id=1, source_target_pairs={{4,8},{8,4},{12,16},{16,12},{20,24},{24,20},{28,0},{0,28},{5,9},{9... | collective-permute-start | bytes 61448 | tf_op jit(solution)/shard_map/ppermute | solution.py:616
  15.9 2.7 %collective-permute-start.2 = (f32[40,128]{1,0:T(8,128)S(1)}, f32[40,128]{1,0:T(8,128)S(1)}, u32[]{:S(2)}, u32[]{:S(2)}) collective-permute-start(f32[40,128]{1,0:T(8,128)S(1)} %get-tuple-element.19._), channel_id=1, source_target_pairs={{0,4},{4,0},{8,12},{12,8},{16,20},{20,16},{24,28},{28,24},{1,5},{5... | collective-permute-start | bytes 61448 | tf_op jit(solution)/shard_map/ppermute | solution.py:615
  30.0 10.7 %all-to-all-start.1 = ((f32[8,8,128]{2,1,0:T(8,128)}), f32[8,8,128]{2,1,0:T(8,128)S(1)}, u32[]{:S(2)}, u32[]{:S(2)}) async-start(f32[8,8,128]{2,1,0:T(8,128)} %get-tuple-element.24), calls=%async_computation.1 | async-start | bytes 65536 | tf_op jit(solution)/shard_map/all_to_all | solution.py:678
